TPU v7x, 32 devices: a whole 2x2x4 slice. The times are simulated.
32 devices in a mesh: groups: 2 (over x), tensor: 16 (over z, y, core).
Axes of the slice: x: 2, y: 2, z: 4, core: 2. Of those that a mesh axis runs over, the one named last changes fastest.
Arguments:
- up_inputs: bfloat16 [32, 128, 8192], P('groups', None, 'tensor'), parts along dimension 0, may hold values from -6 to 6
- up_grads: bfloat16 [32, 128, 28672], P('groups', None, 'tensor'), parts along dimension 0, may hold values from -6 to 6
- down_inputs: bfloat16 [32, 128, 28672], P('groups', None, 'tensor'), parts along dimension 0, may hold values from -6 to 6
- down_grads: bfloat16 [32, 128, 8192], P('groups', None, 'tensor'), parts along dimension 0, may hold values from -6 to 6
- token_counts: int32 [32], P(('groups', 'tensor')), parts along dimension 0, may hold values from 32 to 128, as said below
- pad_offsets: int32 [32], P(('groups', 'tensor')), parts along dimension 0, may hold values from 0 to 96
- sketch_in_up: bfloat16 [8192, 64], P('tensor'), may hold values from -0.0625 to 0.0625
- sketch_out_up: bfloat16 [28672, 64], P('tensor'), may hold values from -0.03125 to 0.03125
- sketch_in_down: bfloat16 [28672, 64], P('tensor'), may hold values from -0.03125 to 0.03125
- sketch_out_down: bfloat16 [8192, 64], P('tensor'), may hold values from -0.0625 to 0.0625
- queries: bfloat16 [64, 8192], P('tensor'), may hold values from -0.0078125 to 0.0078125
Outputs:
- scores: float32 [32, 64], P(('groups', 'tensor')), parts along dimension 0
There are 2 independent parts, one for each index of `groups`. A program takes and returns all parts, laid end to end along the dimension named above; an argument that names none is the same for every part. Nothing has to cross between parts.
Inputs may be any that keep to these rules, and one draw needn't show every extreme that they name: token_counts[e] + pad_offsets[e] <= 128; some example has all 128 slots live.
All inputs are finite; a program needn't handle non-finite values.
Results may differ from a plain program's by a relative error of at most 0.0029.
Values may be sent and summed in bfloat16 or wider, within the bound.
A program may use at most 128 MiB of HBM per device.

v0:
```python
import jax
import jax.numpy as jnp
from jax import lax
from jax.sharding import PartitionSpec as P


def project(acts, grads, p_in, p_out):
    ex, sl, _ = acts.shape
    outs = jnp.dot(grads.reshape(ex * sl, -1), p_out, preferred_element_type=jnp.float32)
    ins = jnp.dot(acts.reshape(ex * sl, -1), p_in, preferred_element_type=jnp.float32)
    return jnp.concatenate([outs, ins], axis=1).reshape(ex, sl, -1)


def outer_sum(proj, live):
    width = proj.shape[2] // 2
    outs = proj[:, :, :width] * live[:, :, None]
    ins = proj[:, :, width:]
    sk = jnp.einsum("esi,esj->eij", outs, ins, precision=lax.Precision.HIGHEST)
    return sk.reshape(proj.shape[0], width * width)


def local(
    up_inputs,
    up_grads,
    down_inputs,
    down_grads,
    token_counts,
    pad_offsets,
    sketch_in_up,
    sketch_out_up,
    sketch_in_down,
    sketch_out_down,
    queries,
):
    seq_len = up_inputs.shape[1]
    slots = jnp.arange(seq_len, dtype=jnp.int32)[None, :]
    live = (
        (slots >= pad_offsets[:, None]) & (slots < pad_offsets[:, None] + token_counts[:, None])
    ).astype(jnp.float32)
    first = project(up_inputs, up_grads, sketch_in_up, sketch_out_up)
    second = project(down_inputs, down_grads, sketch_in_down, sketch_out_down)
    owned_first, owned_second = (
        lax.psum_scatter(first, "tensor", scatter_dimension=0, tiled=True),
        lax.psum_scatter(second, "tensor", scatter_dimension=0, tiled=True),
    )
    train = jnp.concatenate(
        [outer_sum(owned_first, live), outer_sum(owned_second, live)], axis=1
    ).astype(jnp.bfloat16)
    return lax.dot_general(
        train,
        lax.all_gather(queries, "tensor", axis=0, tiled=True),
        (((1,), (1,)), ((), ())),
        preferred_element_type=jnp.float32,
    )


def solution(mesh):
    return jax.shard_map(
        local,
        mesh=mesh,
        in_specs=(
            P("groups", None, "tensor"),
            P("groups", None, "tensor"),
            P("groups", None, "tensor"),
            P("groups", None, "tensor"),
            P(("groups", "tensor")),
            P(("groups", "tensor")),
            P("tensor", None),
            P("tensor", None),
            P("tensor", None),
            P("tensor", None),
            P("tensor", None),
        ),
        out_specs=P(("groups", "tensor"), None),
        check_vma=False,
    )
```

profile of v0, /device:TPU:0, one launch (start us, length us, event | category | flops | bytes accessed | tf_op | source)
XLA Modules:
  0.0 183.1 jit_solution(2428419449679896134)
XLA Ops:
  6.5 0.0 copy-start
  6.5 0.0 copy-start.1
  6.6 5.5 %fusion.6 = f32[2048,64]{0,1:T(8,128)S(1)} fusion(bf16[2048,1792]{1,0:T(8,128)(2,1)} %bitcast.34, bf16[1792,64]{0,1:T(8,128)(2,1)} %param.18), kind=kOutput, calls=%fused_computation.14 | convolution fusion | flops 469762048 | bytes 8093696 | tf_op jit(solution)/shard_map/dot_general | solution.py:9
  12.1 0.7 fusion.7
  12.9 0.1 pad_maximum_fusion
  13.0 1.3 copy.14
  14.3 0.0 reduce-scatter.3.cloned.1.call-update
  14.3 0.0 reduce-scatter.5.cloned.1.call-start
  14.4 2.3 %fusion.8 = f32[2048,64]{0,1:T(8,128)S(1)} fusion(bf16[2048,512]{1,0:T(8,128)(2,1)} %bitcast.38, bf16[512,64]{0,1:T(8,128)(2,1)S(1)} %copy-done.3), kind=kOutput, calls=%fused_computation.16 | convolution fusion | flops 134217728 | bytes 2686976 | tf_op jit(solution)/shard_map/dot_general | solution.py:9
  16.7 5.4 %fusion.9 = f32[2048,64]{0,1:T(8,128)S(1)} fusion(bf16[2048,1792]{1,0:T(8,128)(2,1)} %bitcast.35, bf16[1792,64]{0,1:T(8,128)(2,1)S(1)} %copy-done.1), kind=kOutput, calls=%fused_computation.17 | convolution fusion | flops 469762048 | bytes 8093696 | tf_op jit(solution)/shard_map/dot_general | solution.py:10
  22.1 0.1 pad_maximum_fusion.1
  22.2 1.4 copy.15
  23.6 0.0 reduce-scatter.5.cloned.1.call-update
  23.6 0.0 all-gather.3.cloned.1.call-start
  23.7 0.7 all-gather.3.cloned.1.call-update
  25.7 49.0 %reduce-scatter.3.cloned.1.call-done = f32[1,128,128]{2,1,0:T(8,128)} async-done(((f32[16,128,128]{2,1,0:T(8,128)}), f32[1,128,128]{2,1,0:T(8,128)}) %reduce-scatter.3.cloned.1.call-update) | async-done | bytes 65552 | tf_op jit(solution)/shard_map/reduce_scatter | solution.py:43
  74.6 1.2 convolution_convert_fusion.1
  75.9 0.1 concatenate.18
  76.0 59.2 %reduce-scatter.5.cloned.1.call-done = f32[1,128,128]{2,1,0:T(8,128)} async-done(((f32[16,128,128]{2,1,0:T(8,128)}), f32[1,128,128]{2,1,0:T(8,128)}) %reduce-scatter.5.cloned.1.call-update) | async-done | bytes 65552 | tf_op jit(solution)/shard_map/reduce_scatter | solution.py:44
  135.2 1.2 convolution_convert_fusion
  136.4 0.1 concatenate.20
  136.6 37.7 %all-gather.3.cloned.1.call-done = bf16[16,4,8192]{2,1,0:T(4,128)(2,1)} async-done(((bf16[1,4,8192]{2,1,0:T(4,128)(2,1)}), bf16[16,4,8192]{2,1,0:T(4,128)(2,1)}) %all-gather.3.cloned.1.call-update) | async-done | bytes 1048592 | tf_op jit(solution)/shard_map/all_gather | solution.py:51
  174.3 1.3 reshape.87
  175.6 0.9 fusion.10
  (10 shorter events, 0.0 us)
Async XLA Ops:
  6.5 5.6 %copy-start = (bf16[16,128,512]{2,1,0:T(8,128)(2,1)S(1)}, bf16[16,128,512]{2,1,0:T(8,128)(2,1)}, u32[]{:S(2)}) copy-start(bf16[16,128,512]{2,1,0:T(8,128)(2,1)} %param.11) | copy-start | bytes 6291460
  6.5 5.6 %copy-start.2 = (bf16[512,64]{0,1:T(8,128)(2,1)S(1)}, bf16[512,64]{0,1:T(8,128)(2,1)}, u32[]{:S(2)}) copy-start(bf16[512,64]{0,1:T(8,128)(2,1)} %param.17) | copy-start | bytes 196612
  6.5 68.1 %reduce-scatter.3.cloned.1.call-start = ((), (), s32[]{:S(2)}) async-start(), calls=%async_computation.2 | async-start | bytes 1114112 | tf_op jit(solution)/shard_map/reduce_scatter | solution.py:43
  6.5 7.8 %copy-start.3 = (bf16[512,64]{0,1:T(8,128)(2,1)S(1)}, bf16[512,64]{0,1:T(8,128)(2,1)}, u32[]{:S(2)}) copy-start(bf16[512,64]{0,1:T(8,128)(2,1)} %param.20) | copy-start | bytes 196612
  6.5 10.2 %copy-start.1 = (bf16[1792,64]{0,1:T(8,128)(2,1)S(1)}, bf16[1792,64]{0,1:T(8,128)(2,1)}, u32[]{:S(2)}) copy-start(bf16[1792,64]{0,1:T(8,128)(2,1)} %param.19) | copy-start | bytes 688132
  14.3 120.9 %reduce-scatter.5.cloned.1.call-start = ((), (), s32[]{:S(2)}) async-start(), calls=%async_computation.3 | async-start | bytes 1114112 | tf_op jit(solution)/shard_map/reduce_scatter | solution.py:44
  23.6 150.7 %all-gather.3.cloned.1.call-start = ((), (), s32[]{:S(2)}) async-start(), calls=%async_computation.4 | async-start | bytes 1114112 | tf_op jit(solution)/shard_map/all_gather | solution.py:51
Sparse Core Ops, SparseCore 0:
  14.4 60.1 reduce-scatter.2
  78.7 56.4 reduce-scatter.4
  137.4 36.9 all-gather.2
where the time goes:
time: 183 us
  waiting for transfers between devices  147 us (80%)
  matrix products  17.4 us (10%)
  between operations  14.5 us (8%)
  local copies, waits for them, and re-layouts  4.24 us (2%)
    reduce_scatter x1, waiting for transfers between devices, local(): lax.psum_scatter(second, 'tensor', scatter_dimension=0, tiled=True)  59.2 us
    reduce_scatter x1, waiting for transfers between devices, local(): lax.psum_scatter(first, 'tensor', scatter_dimension=0, tiled=True)  49 us
    all_gather x1, waiting for transfers between devices, local(): lax.all_gather(queries, 'tensor', axis=0, tiled=True)  37.7 us
    dot_general x2, matrix products, project(): jnp.dot(grads.reshape(ex * sl, -1), p_out, preferred_element_type=jnp.flo...  7.87 us
    dot_general x2, matrix products, project(): jnp.dot(acts.reshape(ex * sl, -1), p_in, preferred_element_type=jnp.float32)  6.16 us
  transfers between devices with their start and end apart: 3, of which 3 were waited for; matrix products, arithmetic and copies ran while one was open for 6% of the time, Pallas kernels for 0%

commit v1 on v0

v1 whole, which is shorter than its diff:
```python
import functools

import jax
import jax.numpy as jnp
from jax import lax
from jax.experimental import pallas as pl
from jax.experimental.pallas import tpu as pltpu
from jax.sharding import PartitionSpec as P

Y_TYPE = jnp.bfloat16
Z_TYPE = jnp.float32
MESH = pl.DeviceIdType.MESH
F32 = jnp.float32


def kernel(
    nz,
    upi, upg, dni, dng, cnt, off, siu, sou, sid, sod, q, out,
    v_upi, v_upg, v_dni, v_dng, r_siu, r_sou, r_sid, r_sod, w_out, w_in,
    csend, crecv, own, ysend, yrecv, zsend, zrecv, qraw, qf, qall, sk, acc,
    in_sem, w_sem, q_sem, c_ss, c_rs, y_ss, y_rs, z_ss, z_rs, qz_ss, qz_rs, qx_ss, qx_rs,
):
    g = lax.axis_index("groups")
    me = lax.axis_index("tensor")
    c = lax.rem(me, 2)
    y = lax.rem(me // 2, 2)
    z = me // 4
    kd = upi.shape[2]
    kf = upg.shape[2]
    r = siu.shape[1]
    seq = upi.shape[1]
    nqd = q.shape[0]
    tiles = q.shape[1] // 128

    def at(zz, yy, cc):
        return (g, (zz * 2 + yy) * 2 + cc)

    def zline(j):
        return lax.rem(z + 1 + j, nz)

    q_copy = pltpu.make_async_copy(q, qraw, q_sem)
    q_copy.start()
    w_copies = [
        pltpu.make_async_copy(a, b, w_sem.at[i])
        for i, (a, b) in enumerate(((sou, r_sou), (sod, r_sod), (siu, r_siu), (sid, r_sid)))
    ]
    for w in w_copies:
        w.start()
    loads = []
    for s in range(nz):
        for h in range(2):
            for yy in range(2):
                p = s * 4 + h * 2 + yy
                e = (zline(s) * 2 + (y if yy else 1 - y)) * 2 + (c if h else 1 - c)
                group = [
                    pltpu.make_async_copy(a.at[e], b.at[p], in_sem.at[p, i])
                    for i, (a, b) in enumerate(((upg, v_upg), (dng, v_dng), (upi, v_upi), (dni, v_dni)))
                ]
                for x in group:
                    x.start()
                loads.append(group)

    barrier = pltpu.get_barrier_semaphore()
    pl.semaphore_signal(barrier, inc=1, device_id=at(z, y, 1 - c), device_id_type=MESH)
    pl.semaphore_signal(barrier, inc=1, device_id=at(z, 1 - y, c), device_id_type=MESH)
    for j in range(nz - 1):
        pl.semaphore_signal(barrier, inc=1, device_id=at(zline(j), y, c), device_id_type=MESH)

    q_copy.wait()
    for m in range(tiles):
        qf[pl.ds(m, nqd, stride=tiles), :] = qraw[:, m * 128 : (m + 1) * 128].astype(F32)
    qall[c, y, z] = qf[...].astype(jnp.bfloat16)

    pl.semaphore_wait(barrier, nz + 1)

    q_z = []
    for j in range(nz - 1):
        copy = pltpu.make_async_remote_copy(
            src_ref=qall.at[c, y, z], dst_ref=qall.at[c, y, z],
            send_sem=qz_ss.at[j], recv_sem=qz_rs.at[j],
            device_id=at(zline(j), y, c), device_id_type=MESH,
        )
        copy.start()
        q_z.append(copy)

    for w in w_copies:
        w.wait()
    w_out[:kf, :] = jnp.concatenate([r_sou[...], jnp.zeros((kf, r), jnp.bfloat16)], axis=1)
    w_out[kf:, :] = jnp.concatenate([jnp.zeros((kd, r), jnp.bfloat16), r_sod[...]], axis=1)
    w_in[:kd, :] = jnp.concatenate([r_siu[...], jnp.zeros((kd, r), jnp.bfloat16)], axis=1)
    w_in[kd:, :] = jnp.concatenate([jnp.zeros((kf, r), jnp.bfloat16), r_sid[...]], axis=1)

    c_copies, y_copies, z_copies = [], [], []

    def finish(s):
        y_copies[s].wait_recv()
        total = own[s, 1] + yrecv[s].astype(F32)
        if s == nz - 1:
            return total
        zsend[s] = total.astype(Z_TYPE)
        copy = pltpu.make_async_remote_copy(
            src_ref=zsend.at[s], dst_ref=zrecv.at[s],
            send_sem=z_ss.at[s], recv_sem=z_rs.at[s],
            device_id=at(zline(s), y, c), device_id_type=MESH,
        )
        copy.start()
        z_copies.append(copy)
        return None

    q_y = pltpu.make_async_remote_copy(
        src_ref=qall.at[c, y], dst_ref=qall.at[c, y],
        send_sem=qx_ss.at[0], recv_sem=qx_rs.at[0],
        device_id=at(z, 1 - y, c), device_id_type=MESH,
    )
    q_c = pltpu.make_async_remote_copy(
        src_ref=qall.at[c], dst_ref=qall.at[c],
        send_sem=qx_ss.at[1], recv_sem=qx_rs.at[1],
        device_id=at(z, y, 1 - c), device_id_type=MESH,
    )

    for s in range(nz):
        for h in range(2):
            p = s * 4 + h * 2
            for group in loads[p : p + 2]:
                for x in group:
                    x.wait()

            def dot(v, w):
                return jnp.dot(v[p : p + 2].reshape(2 * seq, -1), w, preferred_element_type=F32)

            outs = dot(v_upg, w_out[:kf, :]) + dot(v_dng, w_out[kf:, :])
            ins = dot(v_upi, w_in[:kd, :]) + dot(v_dni, w_in[kd:, :])
            dst = own if h else csend
            for yy in range(2):
                dst[s, yy, :, :128] = outs[yy * seq : (yy + 1) * seq]
                dst[s, yy, :, 128:] = ins[yy * seq : (yy + 1) * seq]
            if h == 0:
                copy = pltpu.make_async_remote_copy(
                    src_ref=csend.at[s], dst_ref=crecv.at[s],
                    send_sem=c_ss.at[s], recv_sem=c_rs.at[s],
                    device_id=at(z, y, 1 - c), device_id_type=MESH,
                )
                copy.start()
                c_copies.append(copy)
        c_copies[s].wait_recv()
        ysend[s] = (own[s, 0] + crecv[s, 0]).astype(Y_TYPE)
        copy = pltpu.make_async_remote_copy(
            src_ref=ysend.at[s], dst_ref=yrecv.at[s],
            send_sem=y_ss.at[s], recv_sem=y_rs.at[s],
            device_id=at(z, 1 - y, c), device_id_type=MESH,
        )
        copy.start()
        y_copies.append(copy)
        own[s, 1] = own[s, 1] + crecv[s, 1]
        if s == 1:
            for copy in q_z:
                copy.wait_recv()
            q_y.start()
        if s == 2:
            q_y.wait_recv()
            q_c.start()
        if s >= 1:
            finish(s - 1)

    total = finish(nz - 1)
    for s in range(nz - 1):
        z_copies[s].wait_recv()
        total = total + zrecv[s].astype(F32)

    slot = lax.broadcasted_iota(jnp.int32, (seq, 128), 0)
    first = off[0]
    live = (slot >= first) & (slot < first + cnt[0])
    outs = jnp.where(live, total[:, :128], 0.0)
    sk[...] = lax.dot_general(
        outs, total[:, 128:], (((0,), (0,)), ((), ())),
        precision=lax.Precision.HIGHEST, preferred_element_type=F32,
    )
    half = tiles // 2
    lane = lax.broadcasted_iota(jnp.int32, (half, 128), 1)
    even = sk[pl.ds(0, tiles, stride=2), :]
    odd = sk[pl.ds(1, tiles, stride=2), :]
    train = jnp.concatenate(
        [
            jnp.where(lane < r, even[:half], pltpu.roll(odd[:half], r, 1)),
            jnp.where(lane < r, pltpu.roll(even[half:], r, 1), odd[half:]),
        ],
        axis=0,
    )

    q_c.wait_recv()
    at_row = 0
    for zz in range(nz):
        for yy in range(2):
            for cc in range(2):
                rows = qall[cc, yy, zz].astype(F32).reshape(nqd, tiles, 128)
                acc[at_row : at_row + nqd, :] = jnp.sum(rows * train[None], axis=1)
                at_row += nqd
    out[...] = lax.dot_general(
        jnp.ones((8, 128), F32), acc[...], (((1,), (1,)), ((), ())),
        precision=lax.Precision.HIGHEST, preferred_element_type=F32,
    )[:1]

    for copy in q_z + c_copies + y_copies + z_copies + [q_y, q_c]:
        copy.wait_send()


def local(nz, upi, upg, dni, dng, cnt, off, siu, sou, sid, sod, q):
    ex, seq, kd = upi.shape
    kf = upg.shape[2]
    r = siu.shape[1]
    nqd, width = q.shape
    n = 4 * nz
    bf = jnp.bfloat16
    any_ = pl.BlockSpec(memory_space=pl.ANY)
    smem = pl.BlockSpec(memory_space=pltpu.SMEM)
    dma = pltpu.SemaphoreType.DMA
    return pl.pallas_call(
        functools.partial(kernel, nz),
        out_shape=jax.ShapeDtypeStruct((1, nqd * n), F32),
        in_specs=[any_] * 4 + [smem] * 2 + [any_] * 5,
        out_specs=pl.BlockSpec(memory_space=pltpu.VMEM),
        scratch_shapes=[
            pltpu.VMEM((ex, seq, kd), bf),
            pltpu.VMEM((ex, seq, kf), bf),
            pltpu.VMEM((ex, seq, kf), bf),
            pltpu.VMEM((ex, seq, kd), bf),
            pltpu.VMEM((kd, r), bf),
            pltpu.VMEM((kf, r), bf),
            pltpu.VMEM((kf, r), bf),
            pltpu.VMEM((kd, r), bf),
            pltpu.VMEM((kf + kd, 2 * r), bf),
            pltpu.VMEM((kf + kd, 2 * r), bf),
            pltpu.VMEM((nz, 2, seq, 4 * r), F32),
            pltpu.VMEM((nz, 2, seq, 4 * r), F32),
            pltpu.VMEM((nz, 2, seq, 4 * r), F32),
            pltpu.VMEM((nz, seq, 4 * r), Y_TYPE),
            pltpu.VMEM((nz, seq, 4 * r), Y_TYPE),
            pltpu.VMEM((nz, seq, 4 * r), Z_TYPE),
            pltpu.VMEM((nz, seq, 4 * r), Z_TYPE),
            pltpu.VMEM((nqd, width), bf),
            pltpu.VMEM((nqd * width // 128, 128), F32),
            pltpu.VMEM((2, 2, nz, nqd * width // 128, 128), bf),
            pltpu.VMEM((2 * r, 2 * r), F32),
            pltpu.VMEM((nqd * n, 128), F32),
            dma((ex, 4)),
            dma((4,)),
            dma(()),
            dma((nz,)),
            dma((nz,)),
            dma((nz,)),
            dma((nz,)),
            dma((nz,)),
            dma((nz,)),
            dma((nz,)),
            dma((nz,)),
            dma((2,)),
            dma((2,)),
        ],
        compiler_params=pltpu.CompilerParams(
            collective_id=0, has_side_effects=True, vmem_limit_bytes=50 * 1024 * 1024
        ),
    )(upi, upg, dni, dng, cnt, off, siu, sou, sid, sod, q)


def solution(mesh):
    return jax.shard_map(
        functools.partial(local, mesh.shape["tensor"] // 4),
        mesh=mesh,
        in_specs=(
            P("groups", None, "tensor"),
            P("groups", None, "tensor"),
            P("groups", None, "tensor"),
            P("groups", None, "tensor"),
            P(("groups", "tensor")),
            P(("groups", "tensor")),
            P("tensor", None),
            P("tensor", None),
            P("tensor", None),
            P("tensor", None),
            P("tensor", None),
        ),
        out_specs=P(("groups", "tensor"), None),
        check_vma=False,
    )
```

time: 183 us -> 41.6 us (0.23)
  waiting for transfers between devices: 147 us -> 0 us
  Pallas kernels: 0 us -> 32.6 us
  matrix products: 17.4 us -> 0 us
  between operations: 14.5 us -> 1.34 us
  local copies, waits for them, and re-layouts: 4.24 us -> 7.28 us
    reduce_scatter x2 -> x0, waiting for transfers between devices: 108 us -> none  [the longest x1 59.2 us: local(): lax.psum_scatter(second, 'tensor', scatter_dimension=0, tiled=True)]
    all_gather x1 -> x0, waiting for transfers between devices: 37.7 us -> none  [local(): lax.all_gather(queries, 'tensor', axis=0, tiled=True)]
    pallas_call x0 -> x1, Pallas kernels: none -> 32.6 us  [local(): pl.pallas_call(functools.partial(kernel, nz), out_shape=jax.ShapeDtypeStr...]
    dot_general x7 -> x0, matrix products: 17.4 us -> none  [the longest x2 7.87 us: project(): jnp.dot(grads.reshape(ex * sl, -1), p_out, preferred_element_type=jnp.flo...]
    unnamed x9, local copies, waits for them, and re-layouts: 1.35 us -> 7.28 us
    reshape x2 -> x0, local copies, waits for them, and re-layouts: 2.69 us -> none  [project(): return jnp.concatenate([outs, ins], axis=1).reshape(ex, sl, -1)]
  transfers between devices with their start and end apart: 3 -> 0, of which waited for: 3 -> 0; matrix products, arithmetic and copies ran while one was open for 6% -> 0% of each run, Pallas kernels for 0% -> 0%
where the time goes in v1:
time: 41.6 us; the launch traced here: 41.2 us
  Pallas kernels  32.6 us (78%)
  local copies, waits for them, and re-layouts  7.28 us (18%)
  between operations  1.34 us (3%)
    pallas_call x1, Pallas kernels, local(): pl.pallas_call(functools.partial(kernel, nz), out_shape=jax.ShapeDtypeStr...  32.6 us
    unnamed x9, local copies, waits for them, and re-layouts  7.28 us

profile of v1, /device:TPU:0, one launch (start us, length us, event | category | flops | bytes accessed | tf_op | source)
XLA Modules:
  0.0 41.2 jit_solution(745252445027747402)
XLA Ops:
  1.3 1.0 %copy.12.siu = bf16[512,64]{1,0:T(8,128)(2,1)S(1)} copy(bf16[512,64]{0,1:T(8,128)(2,1)} %param.17) | data formatting | bytes 131072 | tf_op args[6]
  2.3 1.0 %copy.15.sod = bf16[512,64]{1,0:T(8,128)(2,1)S(1)} copy(bf16[512,64]{0,1:T(8,128)(2,1)} %param.20) | data formatting | bytes 131072 | tf_op args[9]
  3.2 1.2 %copy.13.sou = bf16[1792,64]{1,0:T(8,128)(2,1)S(1)} copy(bf16[1792,64]{0,1:T(8,128)(2,1)} %param.18) | data formatting | bytes 458752 | tf_op args[7]
  4.4 1.2 %copy.14.sid = bf16[1792,64]{1,0:T(8,128)(2,1)S(1)} copy(bf16[1792,64]{0,1:T(8,128)(2,1)} %param.19) | data formatting | bytes 458752 | tf_op args[8]
  5.7 0.0 copy-start
  5.7 1.6 %copy-done = bf16[16,128,512]{2,1,0:T(8,128)(2,1)S(1)} copy-done((bf16[16,128,512]{2,1,0:T(8,128)(2,1)S(1)}, bf16[16,128,512]{2,1,0:T(8,128)(2,1)}, u32[]{:S(2)}) %copy-start) | copy-done | bytes 2097176
  7.3 0.0 copy-start.1
  7.3 0.8 %copy-done.1 = bf16[4,8192]{1,0:T(4,128)(2,1)S(1)} copy-done((bf16[4,8192]{1,0:T(4,128)(2,1)S(1)}, bf16[4,8192]{1,0:T(4,128)(2,1)}, u32[]{:S(2)}) %copy-start.1) | copy-done | bytes 65560
  8.1 32.6 %shard_map.109 = f32[1,64]{1,0:T(1,128)S(1)} custom-call(bf16[16,128,512]{2,1,0:T(8,128)(2,1)S(1)} %copy-done, bf16[16,128,1792]{2,1,0:T(8,128)(2,1)} %upg.1, bf16[16,128,1792]{2,1,0:T(8,128)(2,1)} %dni.1, bf16[16,128,512]{2,1,0:T(8,128)(2,1)} %dng.1, s32[1]{0:T(128)S(6)} %copy.17.cnt, s32[1]{0:T(128)S(6)} %copy.18.off, bf16[512,64]{1,0:T(8,128)(2,1)S(1)} %copy.12.siu, ...), custom_call_target="tpu_custom_call" | custom-call | tf_op jit(solution)/shard_map/pallas_call | solution.py:217
  40.7 0.5 %copy.19 = f32[1,64]{1,0:T(1,128)} copy(f32[1,64]{1,0:T(1,128)S(1)} %shard_map.109) | data formatting | bytes 512
Async XLA Ops:
  5.7 1.6 %copy-start = (bf16[16,128,512]{2,1,0:T(8,128)(2,1)S(1)}, bf16[16,128,512]{2,1,0:T(8,128)(2,1)}, u32[]{:S(2)}) copy-start(bf16[16,128,512]{2,1,0:T(8,128)(2,1)} %upi.1) | copy-start | bytes 6291460
  7.3 0.8 %copy-start.1 = (bf16[4,8192]{1,0:T(4,128)(2,1)S(1)}, bf16[4,8192]{1,0:T(4,128)(2,1)}, u32[]{:S(2)}) copy-start(bf16[4,8192]{1,0:T(4,128)(2,1)} %q.1) | copy-start | bytes 196612

commit v2 on v1

--- a/solution.py
+++ b/solution.py
@@ -9,6 +9,7 @@
 
 Y_TYPE = jnp.bfloat16
 Z_TYPE = jnp.float32
+AHEAD = 2
 MESH = pl.DeviceIdType.MESH
 F32 = jnp.float32
 
@@ -16,9 +17,9 @@
 def kernel(
     nz,
     upi, upg, dni, dng, cnt, off, siu, sou, sid, sod, q, out,
-    v_upi, v_upg, v_dni, v_dng, r_siu, r_sou, r_sid, r_sod, w_out, w_in,
+    v_upi, v_upg, v_dni, v_dng, v_cnt, v_off, w_out, w_in,
     csend, crecv, own, ysend, yrecv, zsend, zrecv, qraw, qf, qall, sk, acc,
-    in_sem, w_sem, q_sem, c_ss, c_rs, y_ss, y_rs, z_ss, z_rs, qz_ss, qz_rs, qx_ss, qx_rs,
+    in_sem, w_sem, q_sem, n_sem, c_ss, c_rs, y_ss, y_rs, z_ss, z_rs, qz_ss, qz_rs, qx_ss, qx_rs,
 ):
     g = lax.axis_index("groups")
     me = lax.axis_index("tensor")
@@ -27,7 +28,7 @@
     z = me // 4
     kd = upi.shape[2]
     kf = upg.shape[2]
-    r = siu.shape[1]
+    r = siu.shape[0]
     seq = upi.shape[1]
     nqd = q.shape[0]
     tiles = q.shape[1] // 128
@@ -35,14 +36,26 @@
     def at(zz, yy, cc):
         return (g, (zz * 2 + yy) * 2 + cc)
 
+    shifts = sorted(range(1, nz), key=lambda k: -min(k, nz - k)) + [nz]
+
     def zline(j):
-        return lax.rem(z + 1 + j, nz)
+        return lax.rem(z + shifts[j], nz)
 
     q_copy = pltpu.make_async_copy(q, qraw, q_sem)
     q_copy.start()
     w_copies = [
         pltpu.make_async_copy(a, b, w_sem.at[i])
-        for i, (a, b) in enumerate(((sou, r_sou), (sod, r_sod), (siu, r_siu), (sid, r_sid)))
+        for i, (a, b) in enumerate(
+            (
+                (sou, w_out.at[:r, :kf]),
+                (sod, w_out.at[r:, kf:]),
+                (siu, w_in.at[:r, :kd]),
+                (sid, w_in.at[r:, kd:]),
+            )
+        )
+    ]
+    n_copies = [
+        pltpu.make_async_copy(a, b, n_sem.at[i]) for i, (a, b) in enumerate(((cnt, v_cnt), (off, v_off)))
     ]
     for w in w_copies:
         w.start()
@@ -56,8 +69,9 @@
                     pltpu.make_async_copy(a.at[e], b.at[p], in_sem.at[p, i])
                     for i, (a, b) in enumerate(((upg, v_upg), (dng, v_dng), (upi, v_upi), (dni, v_dni)))
                 ]
-                for x in group:
-                    x.start()
+                if s < AHEAD:
+                    for x in group:
+                        x.start()
                 loads.append(group)
 
     barrier = pltpu.get_barrier_semaphore()
@@ -65,6 +79,13 @@
     pl.semaphore_signal(barrier, inc=1, device_id=at(z, 1 - y, c), device_id_type=MESH)
     for j in range(nz - 1):
         pl.semaphore_signal(barrier, inc=1, device_id=at(zline(j), y, c), device_id_type=MESH)
+
+    for w in n_copies:
+        w.start()
+    w_out[r:, :kf] = jnp.zeros((r, kf), jnp.bfloat16)
+    w_out[:r, kf:] = jnp.zeros((r, kd), jnp.bfloat16)
+    w_in[r:, :kd] = jnp.zeros((r, kd), jnp.bfloat16)
+    w_in[:r, kd:] = jnp.zeros((r, kf), jnp.bfloat16)
 
     q_copy.wait()
     for m in range(tiles):
@@ -85,10 +106,6 @@
 
     for w in w_copies:
         w.wait()
-    w_out[:kf, :] = jnp.concatenate([r_sou[...], jnp.zeros((kf, r), jnp.bfloat16)], axis=1)
-    w_out[kf:, :] = jnp.concatenate([jnp.zeros((kd, r), jnp.bfloat16), r_sod[...]], axis=1)
-    w_in[:kd, :] = jnp.concatenate([r_siu[...], jnp.zeros((kd, r), jnp.bfloat16)], axis=1)
-    w_in[kd:, :] = jnp.concatenate([jnp.zeros((kf, r), jnp.bfloat16), r_sid[...]], axis=1)
 
     c_copies, y_copies, z_copies = [], [], []
 
@@ -119,6 +136,9 @@
     )
 
     for s in range(nz):
+        for group in loads[4 * (s + AHEAD) : 4 * (s + AHEAD + 1)]:
+            for x in group:
+                x.start()
         for h in range(2):
             p = s * 4 + h * 2
             for group in loads[p : p + 2]:
@@ -126,10 +146,12 @@
                     x.wait()
 
             def dot(v, w):
-                return jnp.dot(v[p : p + 2].reshape(2 * seq, -1), w, preferred_element_type=F32)
-
-            outs = dot(v_upg, w_out[:kf, :]) + dot(v_dng, w_out[kf:, :])
-            ins = dot(v_upi, w_in[:kd, :]) + dot(v_dni, w_in[kd:, :])
+                return lax.dot_general(
+                    v[p : p + 2].reshape(2 * seq, -1), w, (((1,), (1,)), ((), ())), preferred_element_type=F32
+                )
+
+            outs = dot(v_upg, w_out[:, :kf]) + dot(v_dng, w_out[:, kf:])
+            ins = dot(v_upi, w_in[:, :kd]) + dot(v_dni, w_in[:, kd:])
             dst = own if h else csend
             for yy in range(2):
                 dst[s, yy, :, :128] = outs[yy * seq : (yy + 1) * seq]
@@ -142,6 +164,8 @@
                 )
                 copy.start()
                 c_copies.append(copy)
+                if s >= 1:
+                    finish(s - 1)
         c_copies[s].wait_recv()
         ysend[s] = (own[s, 0] + crecv[s, 0]).astype(Y_TYPE)
         copy = pltpu.make_async_remote_copy(
@@ -152,15 +176,13 @@
         copy.start()
         y_copies.append(copy)
         own[s, 1] = own[s, 1] + crecv[s, 1]
-        if s == 1:
+        if s == nz - 2:
             for copy in q_z:
                 copy.wait_recv()
             q_y.start()
-        if s == 2:
+        if s == nz - 1:
             q_y.wait_recv()
             q_c.start()
-        if s >= 1:
-            finish(s - 1)
 
     total = finish(nz - 1)
     for s in range(nz - 1):
@@ -168,8 +190,10 @@
         total = total + zrecv[s].astype(F32)
 
     slot = lax.broadcasted_iota(jnp.int32, (seq, 128), 0)
-    first = off[0]
-    live = (slot >= first) & (slot < first + cnt[0])
+    for w in n_copies:
+        w.wait()
+    first = v_off[0]
+    live = (slot >= first) & (slot < first + v_cnt[0])
     outs = jnp.where(live, total[:, :128], 0.0)
     sk[...] = lax.dot_general(
         outs, total[:, 128:], (((0,), (0,)), ((), ())),
@@ -205,31 +229,29 @@
 
 
 def local(nz, upi, upg, dni, dng, cnt, off, siu, sou, sid, sod, q):
+    siu, sou, sid, sod = siu.T, sou.T, sid.T, sod.T
     ex, seq, kd = upi.shape
     kf = upg.shape[2]
-    r = siu.shape[1]
+    r = siu.shape[0]
     nqd, width = q.shape
     n = 4 * nz
     bf = jnp.bfloat16
-    any_ = pl.BlockSpec(memory_space=pl.ANY)
-    smem = pl.BlockSpec(memory_space=pltpu.SMEM)
+    hbm = pl.BlockSpec(memory_space=pltpu.HBM)
     dma = pltpu.SemaphoreType.DMA
     return pl.pallas_call(
         functools.partial(kernel, nz),
         out_shape=jax.ShapeDtypeStruct((1, nqd * n), F32),
-        in_specs=[any_] * 4 + [smem] * 2 + [any_] * 5,
+        in_specs=[hbm] * 11,
         out_specs=pl.BlockSpec(memory_space=pltpu.VMEM),
         scratch_shapes=[
             pltpu.VMEM((ex, seq, kd), bf),
             pltpu.VMEM((ex, seq, kf), bf),
             pltpu.VMEM((ex, seq, kf), bf),
             pltpu.VMEM((ex, seq, kd), bf),
-            pltpu.VMEM((kd, r), bf),
-            pltpu.VMEM((kf, r), bf),
-            pltpu.VMEM((kf, r), bf),
-            pltpu.VMEM((kd, r), bf),
-            pltpu.VMEM((kf + kd, 2 * r), bf),
-            pltpu.VMEM((kf + kd, 2 * r), bf),
+            pltpu.SMEM((1,), jnp.int32),
+            pltpu.SMEM((1,), jnp.int32),
+            pltpu.VMEM((2 * r, kf + kd), bf),
+            pltpu.VMEM((2 * r, kf + kd), bf),
             pltpu.VMEM((nz, 2, seq, 4 * r), F32),
             pltpu.VMEM((nz, 2, seq, 4 * r), F32),
             pltpu.VMEM((nz, 2, seq, 4 * r), F32),
@@ -245,6 +267,7 @@
             dma((ex, 4)),
             dma((4,)),
             dma(()),
+            dma((2,)),
             dma((nz,)),
             dma((nz,)),
             dma((nz,)),
@@ -257,7 +280,7 @@
             dma((2,)),
         ],
         compiler_params=pltpu.CompilerParams(
-            collective_id=0, has_side_effects=True, vmem_limit_bytes=50 * 1024 * 1024
+            collective_id=0, has_side_effects=True, vmem_limit_bytes=64 * 1024 * 1024 - 65536
         ),
     )(upi, upg, dni, dng, cnt, off, siu, sou, sid, sod, q)
 

time: 41.6 us -> 31.6 us (0.76)
  local copies, waits for them, and re-layouts: 7.28 us -> 1.19 us
  Pallas kernels: 32.6 us -> 28.7 us
    unnamed x9 -> x1, local copies, waits for them, and re-layouts: 7.28 us -> 1.19 us
    pallas_call x1, Pallas kernels: 32.6 us -> 28.7 us  [local(): pl.pallas_call(functools.partial(kernel, nz), out_shape=jax.ShapeDtypeStr...]
where the time goes in v2:
time: 31.6 us; the launch traced here: 31.2 us
  Pallas kernels  28.7 us (91%)
  between operations  1.3 us (4%)
  local copies, waits for them, and re-layouts  1.19 us (4%)
    pallas_call x1, Pallas kernels, local(): pl.pallas_call(functools.partial(kernel, nz), out_shape=jax.ShapeDtypeStr...  28.7 us
    unnamed x1, local copies, waits for them, and re-layouts  1.19 us

profile of v2, /device:TPU:0, one launch (start us, length us, event | category | flops | bytes accessed | tf_op | source)
XLA Modules:
  0.0 31.2 jit_solution(12283524213645733679)
XLA Ops:
  1.3 28.7 %shard_map.109 = f32[1,64]{1,0:T(1,128)} custom-call(bf16[16,128,512]{2,1,0:T(8,128)(2,1)} %upi.1, bf16[16,128,1792]{2,1,0:T(8,128)(2,1)} %upg.1, bf16[16,128,1792]{2,1,0:T(8,128)(2,1)} %dni.1, bf16[16,128,512]{2,1,0:T(8,128)(2,1)} %dng.1, s32[1]{0:T(128)S(6)} %copy.13.cnt, s32[1]{0:T(128)S(6)} %copy.14.off, bf16[64,512]{1,0:T(8,128)(2,1)} %bitcast.6, ...), custom_call_target="tpu_custom_call" | custom-call | tf_op jit(solution)/shard_map/pallas_call | solution.py:241
  30.0 1.2 %copy.15 = f32[1,64]{1,0:T(1,128)} copy(f32[1,64]{1,0:T(1,128)} %shard_map.109) | data formatting | bytes 512
